TPU v7x, 256 devices: a whole 4x4x8 slice. The times are simulated.
256 devices in a mesh: dp: 16 (over x, z_hi, core), ctx: 16 (over z_lo, y).
Axes of the slice: x: 4, y: 4, z: 8 (z_hi: 2, z_lo: 4; z = z_hi * 4 + z_lo), core: 2. Of those that a mesh axis runs over, the one named last changes fastest.
Arguments:
- projected: bfloat16 [16, 2048, 12288], P('dp', 'ctx'), may hold values from -6 to 6
- short_weight: float32 [3, 12288], replicated, may hold values from -3.5 to 3.5
- filter_taps: float32 [2048, 4096], P('dp', 'ctx'), may hold values from -2 to 2
- skip_gain: float32 [4096], P('ctx'), may hold values from -4 to 4
- upstream: bfloat16 [16, 2048, 4096], P('dp', 'ctx'), may hold values from -6 to 6
Outputs:
- mixer_out: bfloat16 [16, 2048, 4096], P('dp', 'ctx')
- filter_gradient: float32 [2048, 4096], P('dp', 'ctx')
All inputs are finite; a program needn't handle non-finite values.
Results may differ from a plain program's by a relative error of at most 0.0057.
Values may be sent and summed in bfloat16 or wider, within the bound.
A program may use at most 192 MiB of HBM per device.

v0:
```python
import functools
import math

import jax
import jax.numpy as jnp
import ml_dtypes
import numpy as np
from jax import lax
from jax.experimental import pallas as pl
from jax.experimental.pallas import tpu as pltpu
from jax.sharding import PartitionSpec as P

SHORT = 3
BLOCK = 256
HALF = 128
F32 = jnp.float32
BF16 = jnp.bfloat16


def split_table(table):
    high = table.astype(ml_dtypes.bfloat16)
    low = (table - high.astype(np.float64)).astype(ml_dtypes.bfloat16)
    return high, low


def make_tables():
    size = 2 * BLOCK
    freq = np.concatenate([np.arange(0, BLOCK, 2), np.arange(1, BLOCK, 2)])
    time = np.arange(BLOCK)
    angle = 2.0 * np.pi * ((freq[:, None] * time[None, :]) % size) / size
    real, imag = np.cos(angle), -np.sin(angle)
    imag[0] = np.where(time % 2 == 0, 1.0, -1.0)
    forward = np.concatenate([real, imag], axis=0)
    weight = np.full((size, 1), 2.0 / size)
    weight[0] = weight[BLOCK] = 1.0 / size
    inverse = (forward * weight).T
    return split_table(forward) + split_table(inverse)


def dot(a, b):
    return jnp.dot(a, b, preferred_element_type=F32)


def kernel(
    proj, weights, taps, skip, upstream, fwd_hi, fwd_lo, inv_hi, inv_lo,
    mixed, taps_grad,
    pack, halo_out, halo_in, halo, gate, outgoing, incoming, all_taps, taps_spec, spec, joint,
    conv_own, conv_in, grad, core_out, core_in, x_out, x_in, z_out, z_in,
    halo_sems, taps_send, taps_recv, part_send, part_recv, conv_send, conv_recv, red_send, red_recv,
):
    ctx, dp = lax.axis_index("ctx"), lax.axis_index("dp")
    ranks = 16
    rows = proj.shape[0]
    width = proj.shape[1] // 3
    blocks = ranks * rows // BLOCK
    x, zh, core = dp // 4, (dp // 2) % 2, dp % 2
    z_mate = dp + 2 - 4 * zh
    core_mate = dp + 1 - 2 * core

    def rotated(step):
        z, y = (ctx // 4 + step // 4) % 4, (ctx % 4 + step % 4) % 4
        return z * 4 + y

    def plane_mate(step):
        return ((x + step // 2) % 4) * 4 + zh * 2 + (core + step % 2) % 2

    barrier = pltpu.get_barrier_semaphore()

    def greet(step, _):
        pl.semaphore_signal(barrier, inc=1, device_id={"ctx": rotated(step)})
        return 0

    def greet_plane(step, _):
        pl.semaphore_signal(barrier, inc=1, device_id={"dp": plane_mate(step)})
        return 0

    lax.fori_loop(1, ranks, greet, 0)
    lax.fori_loop(1, 8, greet_plane, 0)
    pl.semaphore_signal(barrier, inc=1, device_id={"dp": z_mate})

    piece = 3 * width // 8
    for seg in range(8):
        tail = proj[rows - 16 : rows, seg * piece : (seg + 1) * piece].astype(F32)
        pack[2 * seg : 2 * seg + 2, :] = tail[14:16]
    halo_out[...] = pack[...].astype(BF16)
    all_taps[dp] = taps[...].astype(BF16)

    pl.semaphore_wait(barrier, ranks - 1 + 8)

    halo_copy = pltpu.make_async_remote_copy(
        src_ref=halo_out, dst_ref=halo_in, send_sem=halo_sems.at[0], recv_sem=halo_sems.at[1],
        device_id={"ctx": (ctx + 1) % ranks},
    )
    halo_copy.start()

    def taps_copy(block, slot, target):
        return pltpu.make_async_remote_copy(
            src_ref=all_taps.at[block], dst_ref=all_taps.at[block],
            send_sem=taps_send.at[slot], recv_sem=taps_recv.at[block], device_id={"dp": target},
        )

    taps_copy(dp, 0, z_mate).start()

    def send_own(step, _):
        taps_copy(dp, step, plane_mate(step)).start()
        return 0

    lax.fori_loop(1, 8, send_own, 0)

    halo_copy.wait_recv()
    pack[...] = jnp.where(ctx > 0, halo_in[...].astype(F32), 0.0)
    for seg in range(8):
        halo[0:2, seg * piece : (seg + 1) * piece] = pack[2 * seg : 2 * seg + 2, :]

    row = lax.broadcasted_iota(jnp.int32, (rows, 2 * HALF), 0)

    def short_filter(stream, first):
        cols = pl.ds(pl.multiple_of(stream * width + first, 2 * HALF), 2 * HALF)
        here = proj[:, cols].astype(F32)
        older, old = halo[0:1, cols], halo[1:2, cols]
        back_one = jnp.where(row == 0, old, pltpu.roll(here, 1, 0))
        back_two = jnp.where(row == 0, older, jnp.where(row == 1, old, pltpu.roll(here, 2, 0)))
        w = weights[:, cols]
        return w[0:1] * here + w[1:2] * back_one + w[2:3] * back_two

    def part_copy(chunk, step):
        return pltpu.make_async_remote_copy(
            src_ref=outgoing.at[chunk, step], dst_ref=incoming.at[chunk, ctx],
            send_sem=part_send.at[chunk, step], recv_sem=part_recv.at[chunk, ctx],
            device_id={"ctx": rotated(step)},
        )

    def make_parts(first):
        gate_q = short_filter(0, first)
        product = (short_filter(1, first) * short_filter(2, first)).astype(BF16)
        cols = pl.ds(pl.multiple_of(first, 2 * HALF), 2 * HALF)
        gate[:, cols] = gate_q
        cotangent = (upstream[:, cols].astype(F32) * gate_q).astype(BF16)
        return [
            jnp.concatenate([product[:, lane : lane + HALF], cotangent[:, lane : lane + HALF]], axis=1)
            for lane in (0, HALF)
        ]

    def send_part(index, _):
        step = ranks - 1 - index
        parts = make_parts(rotated(step) * 2 * HALF)
        outgoing[0, step] = parts[0]
        outgoing[1, step] = parts[1]
        part_copy(0, step).start()
        return 0

    lax.fori_loop(0, ranks - 1, send_part, 0)

    def send_late(index, _):
        part_copy(1, ranks - 1 - index).start()
        return 0

    lax.fori_loop(0, ranks - 1, send_late, 0)
    parts = make_parts(ctx * 2 * HALF)
    incoming[0, ctx] = parts[0]
    incoming[1, ctx] = parts[1]

    taps_copy(z_mate, 0, z_mate).wait_recv()

    def forward_taps(step, _):
        taps_copy(z_mate, 7 + step, plane_mate(step)).start()
        return 0

    lax.fori_loop(1, 8, forward_taps, 0)

    def await_taps(step, _):
        taps_copy(plane_mate(step), 0, z_mate).wait_recv()
        taps_copy(plane_mate(step) + 2 - 4 * zh, 0, z_mate).wait_recv()
        return 0

    lax.fori_loop(1, 8, await_taps, 0)

    def transform(block):
        return dot(fwd_hi[...], block) + dot(fwd_lo[...], block)

    def taps_transform(index, _):
        taps_spec[index] = transform(all_taps[pl.ds(2 * index, 2)].reshape(BLOCK, 2 * HALF))
        return 0

    lax.fori_loop(0, blocks, taps_transform, 0)

    def conv_copy(chunk, target):
        return pltpu.make_async_remote_copy(
            src_ref=conv_own.at[chunk, target], dst_ref=conv_in.at[ctx, chunk],
            send_sem=conv_send.at[chunk, target], recv_sem=conv_recv.at[ctx, chunk],
            device_id={"ctx": target},
        )

    sublane = lax.broadcasted_iota(jnp.int32, (8, HALF), 0)
    scale = 1.0 / math.sqrt(ranks * ranks * rows)

    for chunk in range(2):
        lanes = slice(chunk * HALF, (chunk + 1) * HALF)

        def part_transform(index, _):
            for source in (2 * index, 2 * index + 1):

                @pl.when(source != ctx)
                def _():
                    pltpu.make_async_remote_copy(
                        src_ref=outgoing.at[chunk, 0], dst_ref=incoming.at[chunk, source],
                        send_sem=part_send.at[chunk, 0], recv_sem=part_recv.at[chunk, source],
                        device_id={"ctx": rotated(1)},
                    ).wait_recv()

            spec[index] = transform(incoming[chunk, pl.ds(2 * index, 2)].reshape(BLOCK, 2 * HALF))
            return 0

        lax.fori_loop(0, blocks, part_transform, 0)

        def mix(tile, _):
            real = pl.ds(pl.multiple_of(tile * 8, 8), 8)
            imag = pl.ds(pl.multiple_of(BLOCK + tile * 8, 8), 8)
            sign = jnp.where(tile < BLOCK // 16, 1.0, -1.0)
            ends = (sublane + tile * 8) == 0
            p_r = [spec[b, real, 0:HALF] for b in range(blocks)]
            p_i = [spec[b, imag, 0:HALF] for b in range(blocks)]

            h_r = [taps_spec[b, real, lanes] for b in range(blocks)]
            h_i = [taps_spec[b, imag, lanes] for b in range(blocks)]
            p_s = [p_r[b] + p_i[b] for b in range(blocks)]
            h_s = [h_r[b] + h_i[b] for b in range(blocks)]
            last = None
            for b in range(blocks):
                rr = sum(p_r[i] * h_r[b - i] for i in range(1, b + 1)) + p_r[0] * h_r[b] if b else p_r[0] * h_r[0]
                ii = sum(p_i[i] * h_i[b - i] for i in range(1, b + 1)) + p_i[0] * h_i[b] if b else p_i[0] * h_i[0]
                ss = sum(p_s[i] * h_s[b - i] for i in range(1, b + 1)) + p_s[0] * h_s[b] if b else p_s[0] * h_s[0]
                now = (rr - jnp.where(ends, 0.0, ii), jnp.where(ends, ii, ss - rr - ii))
                if last is None:
                    joint[b, real, 0:HALF], joint[b, imag, 0:HALF] = now
                else:
                    joint[b, real, 0:HALF] = now[0] + sign * last[0]
                    joint[b, imag, 0:HALF] = now[1] + sign * last[1]
                last = now

            g_r = [spec[b, real, HALF : 2 * HALF] for b in range(blocks)]
            g_i = [spec[b, imag, HALF : 2 * HALF] for b in range(blocks)]
            p_d = [p_r[b] - p_i[b] for b in range(blocks)]
            g_s = [g_r[b] + g_i[b] for b in range(blocks)]
            last = None
            for b in reversed(range(blocks)):
                rr = p_r[0] * g_r[b]
                ii = p_i[0] * g_i[b]
                ss = p_d[0] * g_s[b]
                for i in range(1, blocks - b):
                    rr = rr + p_r[i] * g_r[b + i]
                    ii = ii + p_i[i] * g_i[b + i]
                    ss = ss + p_d[i] * g_s[b + i]
                now = (rr + jnp.where(ends, 0.0, ii), jnp.where(ends, ii, ss - rr + ii))
                if last is None:
                    joint[b, real, HALF : 2 * HALF], joint[b, imag, HALF : 2 * HALF] = now
                else:
                    joint[b, real, HALF : 2 * HALF] = now[0] + sign * last[0]
                    joint[b, imag, HALF : 2 * HALF] = now[1] + sign * last[1]
                last = now
            return 0

        lax.fori_loop(0, BLOCK // 8, mix, 0)

        def back(index, _):
            b = (ctx // 2 + blocks // 2 + index) % blocks
            value = joint[b]
            high = value.astype(BF16)
            low = (value - high.astype(F32)).astype(BF16)
            result = dot(inv_hi[...], high) + dot(inv_hi[...], low) + dot(inv_lo[...], high)
            product = incoming[chunk, pl.ds(2 * b, 2), :, 0:HALF].reshape(BLOCK, HALF).astype(F32)
            conv = (result[:, 0:HALF] + skip[:, lanes] * product).astype(BF16)
            conv_own[chunk, pl.ds(2 * b, 2)] = conv.reshape(2, HALF, HALF)
            grad[pl.ds(2 * b, 2), :, lanes] = (result[:, HALF : 2 * HALF] * scale).reshape(2, HALF, HALF)
            for target in (2 * b, 2 * b + 1):

                @pl.when(target != ctx)
                def _():
                    conv_copy(chunk, target).start()

            return 0

        lax.fori_loop(0, blocks, back, 0)

    def reduce_copy(slot, source, target, device):
        return pltpu.make_async_remote_copy(
            src_ref=source, dst_ref=target, send_sem=red_send.at[slot], recv_sem=red_recv.at[slot],
            device_id={"dp": device},
        )

    core_copy = reduce_copy(0, core_out, core_in, core_mate)
    x_copies = [
        reduce_copy(i, x_out.at[i - 1], x_in.at[i - 1], ((x + i) % 4) * 4 + zh * 2 + core) for i in (1, 2, 3)
    ]
    z_copy = reduce_copy(4, z_out, z_in, z_mate)

    def core_part(index, _):
        core_out[index] = grad[2 * index + 1 - core].astype(BF16)
        return 0

    lax.fori_loop(0, 8, core_part, 0)
    core_copy.start()
    core_copy.wait_recv()

    for i in (1, 2, 3):
        to = (x + i) % 4
        for half in (0, 1):
            j = 2 * to + half
            x_out[i - 1, half] = (grad[2 * j + core] + core_in[j].astype(F32)).astype(BF16)
        x_copies[i - 1].start()
    for copy in x_copies:
        copy.wait_recv()

    def x_total(half):
        j = 2 * x + half
        total = grad[2 * j + core] + core_in[j].astype(F32)
        for i in range(3):
            total = total + x_in[i, half].astype(F32)
        return total

    z_out[...] = x_total(1 - zh).astype(BF16)
    z_copy.start()

    def finish(index, _):
        source = rotated(index)
        for chunk in range(2):
            cols = pl.ds(pl.multiple_of((source * 2 + chunk) * HALF, HALF), HALF)

            @pl.when(source != ctx)
            def _():
                pltpu.make_async_remote_copy(
                    src_ref=conv_own.at[chunk, 0], dst_ref=conv_in.at[source, chunk],
                    send_sem=conv_send.at[chunk, 0], recv_sem=conv_recv.at[source, chunk],
                    device_id={"ctx": rotated(1)},
                ).wait_recv()
                mixed[:, cols] = (gate[:, cols] * conv_in[source, chunk].astype(F32)).astype(BF16)

            @pl.when(source == ctx)
            def _():
                mixed[:, cols] = (gate[:, cols] * conv_own[chunk, source].astype(F32)).astype(BF16)

        return 0

    lax.fori_loop(0, ranks, finish, 0)

    z_copy.wait_recv()
    taps_grad[...] = x_total(zh) + z_in[...].astype(F32)

    halo_copy.wait_send()

    def drain_taps(step, _):
        taps_copy(dp, step, z_mate).wait_send()
        return 0

    lax.fori_loop(0, 15, drain_taps, 0)

    def drain_parts(step, _):
        for chunk in range(2):
            part_copy(chunk, step).wait_send()
            conv_copy(chunk, rotated(step)).wait_send()
        return 0

    lax.fori_loop(1, ranks, drain_parts, 0)
    core_copy.wait_send()
    for copy in x_copies:
        copy.wait_send()
    z_copy.wait_send()


def per_device(projected, short_weight, filter_taps, skip_gain, upstream):
    rows, joined = projected.shape[1:]
    width = joined // 3
    ranks = 16
    lanes = 2 * HALF
    blocks = ranks * rows // BLOCK
    tables = [jnp.asarray(t) for t in make_tables()]
    vmem = pl.BlockSpec(memory_space=pltpu.VMEM)
    mixed, taps_grad = pl.pallas_call(
        kernel,
        out_shape=[
            jax.ShapeDtypeStruct((rows, width), BF16),
            jax.ShapeDtypeStruct((rows, lanes), F32),
        ],
        in_specs=[vmem] * 9,
        out_specs=[vmem] * 2,
        scratch_shapes=[
            pltpu.VMEM((16, joined // 8), F32),
            pltpu.VMEM((16, joined // 8), BF16),
            pltpu.VMEM((16, joined // 8), BF16),
            pltpu.VMEM((8, joined), F32),
            pltpu.VMEM((rows, width), F32),
            pltpu.VMEM((2, ranks, rows, lanes), BF16),
            pltpu.VMEM((2, ranks, rows, lanes), BF16),
            pltpu.VMEM((ranks, rows, lanes), BF16),
            pltpu.VMEM((blocks, 2 * BLOCK, lanes), F32),
            pltpu.VMEM((blocks, 2 * BLOCK, lanes), F32),
            pltpu.VMEM((blocks, 2 * BLOCK, lanes), F32),
            pltpu.VMEM((2, ranks, rows, HALF), BF16),
            pltpu.VMEM((ranks, 2, rows, HALF), BF16),
            pltpu.VMEM((ranks, rows, lanes), F32),
            pltpu.VMEM((8, rows, lanes), BF16),
            pltpu.VMEM((8, rows, lanes), BF16),
            pltpu.VMEM((3, 2, rows, lanes), BF16),
            pltpu.VMEM((3, 2, rows, lanes), BF16),
            pltpu.VMEM((rows, lanes), BF16),
            pltpu.VMEM((rows, lanes), BF16),
            pltpu.SemaphoreType.DMA((2,)),
            pltpu.SemaphoreType.DMA((16,)),
            pltpu.SemaphoreType.DMA((16,)),
            pltpu.SemaphoreType.DMA((2, 16)),
            pltpu.SemaphoreType.DMA((2, 16)),
            pltpu.SemaphoreType.DMA((2, 16)),
            pltpu.SemaphoreType.DMA((16, 2)),
            pltpu.SemaphoreType.DMA((5,)),
            pltpu.SemaphoreType.DMA((5,)),
        ],
        compiler_params=pltpu.CompilerParams(
            collective_id=0, has_side_effects=True, vmem_limit_bytes=56 * 2**20
        ),
    )(
        projected.reshape(rows, joined), short_weight, filter_taps, skip_gain.reshape(1, lanes),
        upstream.reshape(rows, width), *tables,
    )
    return (mixed.reshape(1, rows, width), taps_grad)


def solution(mesh):
    in_specs = (P("dp", "ctx", None), P(), P("dp", "ctx"), P("ctx"), P("dp", "ctx", None))
    out_specs = (P("dp", "ctx", None), P("dp", "ctx"))
    return jax.shard_map(
        per_device, mesh=mesh, in_specs=in_specs, out_specs=out_specs, check_vma=False
    )
```

profile of v0, /device:TPU:1, one launch (start us, length us, event | category | flops | bytes accessed | tf_op | source)
XLA Modules:
  0.0 104.7 jit_solution(16116780136764133209)
XLA Ops:
  0.6 100.2 %shard_map.104 = (bf16[128,4096]{1,0:T(8,128)(2,1)}, f32[128,256]{1,0:T(8,128)}) custom-call(bf16[128,12288]{1,0:T(8,128)(2,1)} %bitcast.4, f32[3,12288]{1,0:T(4,128)} %weights.1, f32[128,256]{1,0:T(8,128)} %taps.1, f32[1,256]{1,0:T(1,128)} %bitcast.7, bf16[128,4096]{1,0:T(8,128)(2,1)} %bitcast.6, bf16[512,256]{1,0:T(8,128)(2,1)} %constant.8.clone.fwd_hi, ...), custom_call_target="tpu_custom_call" | custom-call | tf_op jit(solution)/shard_map/pallas_call | solution.py:378
  100.9 2.3 %copy.13 = bf16[1,128,4096]{2,1,0:T(8,128)(2,1)} copy(bf16[1,128,4096]{2,1,0:T(8,128)(2,1)} %bitcast.5) | data formatting | bytes 2097152
  103.1 1.6 %copy.14 = f32[128,256]{1,0:T(8,128)} copy(f32[128,256]{1,0:T(8,128)} %get-tuple-element.9) | data formatting | bytes 262144
where the time goes:
time: 105 us
  Pallas kernels  100 us (95%)
  local copies, waits for them, and re-layouts  3.85 us (4%)
    pallas_call x1, Pallas kernels, per_device(): pl.pallas_call(kernel, out_shape=[jax.ShapeDtypeStruct((rows, width), BF1...  100 us
    unnamed x2, local copies, waits for them, and re-layouts  3.85 us

commit v1 on v0

v1 whole, which is shorter than its diff:
```python
import functools
import math

import jax
import jax.numpy as jnp
import ml_dtypes
import numpy as np
from jax import lax
from jax.experimental import pallas as pl
from jax.experimental.pallas import tpu as pltpu
from jax.sharding import PartitionSpec as P

SHORT = 3
BLOCK = 256
HALF = 128
WINDOW = 5
F32 = jnp.float32
BF16 = jnp.bfloat16


def split_table(table):
    high = table.astype(ml_dtypes.bfloat16)
    low = (table - high.astype(np.float64)).astype(ml_dtypes.bfloat16)
    return high, low


def make_tables():
    size = 2 * BLOCK
    freq = np.concatenate([np.arange(0, BLOCK, 2), np.arange(1, BLOCK, 2)])
    time = np.arange(BLOCK)
    angle = 2.0 * np.pi * ((freq[:, None] * time[None, :]) % size) / size
    real, imag = np.cos(angle), -np.sin(angle)
    imag[0] = np.where(time % 2 == 0, 1.0, -1.0)
    forward = np.concatenate([real, imag], axis=0)
    weight = np.full((size, 1), 2.0 / size)
    weight[0] = weight[BLOCK] = 1.0 / size
    inverse = (forward * weight).T
    return np.stack(split_table(forward)), np.stack(split_table(inverse))


def dot(a, b):
    return jnp.dot(a, b, preferred_element_type=F32)


def kernel(
    window, proj_hbm, weights, taps, skip, upstream_hbm, forward_hbm, inverse_hbm,
    mixed, taps_grad,
    proj, upstream, forward, inverse, tail, pack, halo_out, halo_in, halo, gate, mixed_own,
    outgoing, incoming, all_taps, taps_spec, spec, joint, conv_own, conv_in, grad,
    core_out, core_in, x_out, x_in, z_out, z_in,
    load_sems, table_sems, store_sems, halo_sems, taps_send, taps_recv, head_send, head_recv,
    part_send, part_recv, conv_send, conv_recv, red_send, red_recv,
):
    ctx, dp = lax.axis_index("ctx"), lax.axis_index("dp")
    ranks, side = 16, 4
    rows = proj.shape[0]
    width = proj.shape[1] // 3
    lanes = 2 * HALF
    blocks = ranks * rows // BLOCK
    z, y = ctx // side, ctx % side
    x, zh, core = dp // 4, (dp // 2) % 2, dp % 2
    z_mate = dp + 2 - 4 * zh
    core_mate = dp + 1 - 2 * core

    def target_of(step):
        return ((z + step // side) % side) * side + (y + step % side) % side

    def source_of(step):
        return ((z + side - step // side) % side) * side + (y + side - step % side) % side

    def plane_mate(step):
        return ((x + step // 2) % 4) * 4 + zh * 2 + (core + step % 2) % 2

    barrier = pltpu.get_barrier_semaphore()

    def greet(step, _):
        pl.semaphore_signal(barrier, inc=1, device_id={"ctx": target_of(step)})
        return 0

    def greet_plane(step, _):
        pl.semaphore_signal(barrier, inc=1, device_id={"dp": plane_mate(step)})
        return 0

    lax.fori_loop(1, ranks, greet, 0)
    lax.fori_loop(1, 8, greet_plane, 0)
    pl.semaphore_signal(barrier, inc=1, device_id={"dp": z_mate})

    group = side * lanes

    def loads_of(far):
        first = ((z + far) % side) * group
        copies = []
        for stream in range(3):
            cols = pl.ds(pl.multiple_of(stream * width + first, group), group)
            copies.append(
                pltpu.make_async_copy(proj_hbm.at[:, cols], proj.at[:, cols], load_sems.at[far, stream])
            )
        cols = pl.ds(pl.multiple_of(first, group), group)
        copies.append(
            pltpu.make_async_copy(upstream_hbm.at[:, cols], upstream.at[:, cols], load_sems.at[far, 3])
        )
        return copies

    tail_load = pltpu.make_async_copy(proj_hbm.at[pl.ds(rows - 16, 16)], tail, table_sems.at[0])
    tail_load.start()
    for far in (3, 2, 1, 0):
        for copy in loads_of(far):
            copy.start()
    table_loads = [
        pltpu.make_async_copy(forward_hbm, forward, table_sems.at[1]),
        pltpu.make_async_copy(inverse_hbm, inverse, table_sems.at[2]),
    ]
    for copy in table_loads:
        copy.start()

    all_taps[dp] = taps[...].astype(BF16)
    tail_load.wait()
    piece = 3 * width // 8
    for seg in range(8):
        last = tail[:, seg * piece : (seg + 1) * piece].astype(F32)
        pack[2 * seg : 2 * seg + 2, :] = last[14:16]
    halo_out[...] = pack[...].astype(BF16)

    pl.semaphore_wait(barrier, ranks - 1 + 8)

    halo_copy = pltpu.make_async_remote_copy(
        src_ref=halo_out, dst_ref=halo_in, send_sem=halo_sems.at[0], recv_sem=halo_sems.at[1],
        device_id={"ctx": (ctx + 1) % ranks},
    )
    halo_copy.start()

    def taps_copy(block, slot, target):
        return pltpu.make_async_remote_copy(
            src_ref=all_taps.at[block], dst_ref=all_taps.at[block],
            send_sem=taps_send.at[slot], recv_sem=taps_recv.at[block], device_id={"dp": target},
        )

    taps_copy(dp, 0, z_mate).start()

    def body_copy(step, landing):
        body = pl.ds(16, rows - 16)
        return pltpu.make_async_remote_copy(
            src_ref=outgoing.at[0, step, body], dst_ref=incoming.at[0, landing, body],
            send_sem=part_send.at[0, step], recv_sem=part_recv.at[0, landing],
            device_id={"ctx": target_of(step)},
        )

    def head_copy(step, landing):
        head = pl.ds(0, 16)
        return pltpu.make_async_remote_copy(
            src_ref=outgoing.at[0, step, head], dst_ref=incoming.at[0, landing, head],
            send_sem=head_send.at[step], recv_sem=head_recv.at[landing],
            device_id={"ctx": target_of(step)},
        )

    def late_copy(step, landing):
        return pltpu.make_async_remote_copy(
            src_ref=outgoing.at[1, step], dst_ref=incoming.at[1, landing],
            send_sem=part_send.at[1, step], recv_sem=part_recv.at[1, landing],
            device_id={"ctx": target_of(step)},
        )

    def conv_copy(chunk, target, landing):
        return pltpu.make_async_remote_copy(
            src_ref=conv_own.at[chunk, target], dst_ref=conv_in.at[landing, chunk],
            send_sem=conv_send.at[chunk, target], recv_sem=conv_recv.at[landing, chunk],
            device_id={"ctx": target},
        )

    def columns(first):
        return pl.ds(pl.multiple_of(first, lanes), lanes)

    def filtered(stream, first):
        cols = columns(stream * width + first)
        here = proj[:, cols].astype(F32)
        w = weights[:, cols]
        return w[0:1] * here + w[1:2] * pltpu.roll(here, 1, 0) + w[2:3] * pltpu.roll(here, 2, 0)

    head_row = lax.broadcasted_iota(jnp.int32, (16, lanes), 0)

    def filtered_head(stream, first):
        cols = columns(stream * width + first)
        here = proj[0:16, cols].astype(F32)
        older, old = halo[0:1, cols], halo[1:2, cols]
        back_one = jnp.where(head_row == 0, old, pltpu.roll(here, 1, 0))
        back_two = jnp.where(head_row == 0, older, jnp.where(head_row == 1, old, pltpu.roll(here, 2, 0)))
        w = weights[:, cols]
        return w[0:1] * here + w[1:2] * back_one + w[2:3] * back_two

    def make_parts(step, count, filter_rows):
        first = target_of(step) * lanes
        gate_q = filter_rows(0, first)
        product = (filter_rows(1, first) * filter_rows(2, first)).astype(BF16)
        cols = columns(first)
        gate[0:count, cols] = gate_q
        cotangent = (upstream[0:count, cols].astype(F32) * gate_q).astype(BF16)
        return [
            jnp.concatenate([product[:, lane : lane + HALF], cotangent[:, lane : lane + HALF]], axis=1)
            for lane in (0, HALF)
        ]

    def send_body(index, _):
        step = ranks - 1 - index
        parts = make_parts(step, rows, filtered)
        outgoing[0, step] = parts[0]
        outgoing[1, step] = parts[1]
        body_copy(step, ctx).start()
        return 0

    for far in (3, 2, 1, 0):
        for copy in loads_of(far):
            copy.wait()
        lax.fori_loop((3 - far) * side, min((4 - far) * side, ranks - 1), send_body, 0)
    parts = make_parts(0, rows, filtered)
    incoming[0, ctx] = parts[0]
    incoming[1, ctx] = parts[1]

    def send_own(step, _):
        taps_copy(dp, step, plane_mate(step)).start()
        return 0

    lax.fori_loop(1, 8, send_own, 0)

    halo_copy.wait_recv()
    pack[...] = jnp.where(ctx > 0, halo_in[...].astype(F32), 0.0)
    for seg in range(8):
        halo[0:2, seg * piece : (seg + 1) * piece] = pack[2 * seg : 2 * seg + 2, :]

    def send_head(index, _):
        step = ranks - 1 - index
        parts = make_parts(step, 16, filtered_head)
        outgoing[0, step, 0:16] = parts[0]
        outgoing[1, step, 0:16] = parts[1]
        head_copy(step, ctx).start()
        return 0

    lax.fori_loop(0, ranks - 1, send_head, 0)
    parts = make_parts(0, 16, filtered_head)
    incoming[0, ctx, 0:16] = parts[0]
    incoming[1, ctx, 0:16] = parts[1]

    def send_late(index, _):
        late_copy(ranks - 1 - index, ctx).start()
        return 0

    def await_body(index, _):
        step = ranks - 1 - (index - window)
        body_copy(step, source_of(step)).wait_recv()
        return 0

    def await_and_send(index, _):
        await_body(index, 0)
        return send_late(index, 0)

    lax.fori_loop(0, window, send_late, 0)

    taps_copy(z_mate, 0, z_mate).wait_recv()

    def forward_taps(step, _):
        taps_copy(z_mate, 7 + step, plane_mate(step)).start()
        return 0

    lax.fori_loop(1, 8, forward_taps, 0)

    lax.fori_loop(window, ranks - 1, await_and_send, 0)

    def await_taps(step, _):
        taps_copy(plane_mate(step), 0, z_mate).wait_recv()
        taps_copy(plane_mate(step) + 2 - 4 * zh, 0, z_mate).wait_recv()
        return 0

    lax.fori_loop(1, 8, await_taps, 0)
    for copy in table_loads:
        copy.wait()

    def transform(block):
        return dot(forward[0], block) + dot(forward[1], block)

    def taps_transform(index, _):
        taps_spec[index] = transform(all_taps[pl.ds(2 * index, 2)].reshape(BLOCK, lanes))
        return 0

    lax.fori_loop(0, blocks, taps_transform, 0)
    lax.fori_loop(ranks - 1, ranks - 1 + window, await_body, 0)

    def await_head(step, _):
        head_copy(step, source_of(step)).wait_recv()
        return 0

    lax.fori_loop(1, ranks, await_head, 0)

    sublane = lax.broadcasted_iota(jnp.int32, (8, HALF), 0)
    scale = 1.0 / math.sqrt(ranks * ranks * rows)

    def part_transform(chunk, index):
        spec[index] = transform(incoming[chunk, pl.ds(2 * index, 2)].reshape(BLOCK, lanes))

    def rows_of(tile):
        real = pl.ds(pl.multiple_of(tile * 8, 8), 8)
        imag = pl.ds(pl.multiple_of(BLOCK + tile * 8, 8), 8)
        sign = jnp.where(tile < BLOCK // 16, 1.0, -1.0)
        return real, imag, sign, (sublane + tile * 8) == 0

    def put(b, real, imag, sign, now, last):
        at = slice((b % 2) * HALF, (b % 2 + 1) * HALF)
        if last is not None:
            joint[b // 2, real, at] = now[0] + sign * last[0]
            joint[b // 2, imag, at] = now[1] + sign * last[1]
        else:
            joint[b // 2, real, at], joint[b // 2, imag, at] = now

    def sum_products(pairs):
        total = None
        for a, b in pairs:
            total = a * b if total is None else total + a * b
        return total

    def mix_conv(chunk):
        own = slice(chunk * HALF, (chunk + 1) * HALF)

        def tile_step(tile, _):
            real, imag, sign, ends = rows_of(tile)
            p_r = [spec[b, real, 0:HALF] for b in range(blocks)]
            p_i = [spec[b, imag, 0:HALF] for b in range(blocks)]
            h_r = [taps_spec[b, real, own] for b in range(blocks)]
            h_i = [taps_spec[b, imag, own] for b in range(blocks)]
            p_s = [p_r[b] + p_i[b] for b in range(blocks)]
            h_s = [h_r[b] + h_i[b] for b in range(blocks)]
            last = None
            for b in range(blocks):
                rr = sum_products((p_r[i], h_r[b - i]) for i in range(b + 1))
                ii = sum_products((p_i[i], h_i[b - i]) for i in range(b + 1))
                ss = sum_products((p_s[i], h_s[b - i]) for i in range(b + 1))
                now = (rr - jnp.where(ends, 0.0, ii), jnp.where(ends, ii, ss - rr - ii))
                put(b, real, imag, sign, now, last)
                last = now
            return 0

        lax.fori_loop(0, BLOCK // 8, tile_step, 0)

    def mix_grad():
        def tile_step(tile, _):
            real, imag, sign, ends = rows_of(tile)
            p_r = [spec[b, real, 0:HALF] for b in range(blocks)]
            p_i = [spec[b, imag, 0:HALF] for b in range(blocks)]
            g_r = [spec[b, real, HALF:lanes] for b in range(blocks)]
            g_i = [spec[b, imag, HALF:lanes] for b in range(blocks)]
            p_d = [p_r[b] - p_i[b] for b in range(blocks)]
            g_s = [g_r[b] + g_i[b] for b in range(blocks)]
            last = None
            for b in reversed(range(blocks)):
                rr = sum_products((p_r[i], g_r[b + i]) for i in range(blocks - b))
                ii = sum_products((p_i[i], g_i[b + i]) for i in range(blocks - b))
                ss = sum_products((p_d[i], g_s[b + i]) for i in range(blocks - b))
                now = (rr + jnp.where(ends, 0.0, ii), jnp.where(ends, ii, ss - rr + ii))
                put(b, real, imag, sign, now, last)
                last = now
            return 0

        lax.fori_loop(0, BLOCK // 8, tile_step, 0)

    def back(pair):
        value = joint[pair]
        high = value.astype(BF16)
        low = (value - high.astype(F32)).astype(BF16)
        return dot(inverse[0], high) + dot(inverse[0], low) + dot(inverse[1], high)

    def back_conv(chunk, send):
        own = slice(chunk * HALF, (chunk + 1) * HALF)

        def pair_step(index, _):
            pair = (z + side - 1 - index) % side
            result = back(pair)
            for part in range(4):
                target = 4 * pair + part
                value = result[(part % 2) * HALF : (part % 2 + 1) * HALF, (part // 2) * HALF : (part // 2 + 1) * HALF]
                product = incoming[chunk, target, :, 0:HALF].astype(F32)
                conv_own[chunk, target] = (value + skip[:, own] * product).astype(BF16)
                if send:

                    @pl.when(target != ctx)
                    def _():
                        conv_copy(chunk, target, ctx).start()

            return 0

        lax.fori_loop(0, side, pair_step, 0)

    def back_grad(chunk):
        def pair_step(pair, _):
            result = back(pair)
            for part in range(4):
                value = result[(part % 2) * HALF : (part % 2 + 1) * HALF, (part // 2) * HALF : (part // 2 + 1) * HALF]
                grad[chunk, 4 * pair + part] = value * scale
            return 0

        lax.fori_loop(0, side, pair_step, 0)

    def reduce_copy(chunk, slot, source, target, device):
        return pltpu.make_async_remote_copy(
            src_ref=source, dst_ref=target, send_sem=red_send.at[chunk, slot],
            recv_sem=red_recv.at[chunk, slot], device_id={"dp": device},
        )

    def core_copy(chunk):
        return reduce_copy(chunk, 0, core_out.at[chunk], core_in.at[chunk], core_mate)

    def x_copy(chunk, i):
        device = ((x + i) % 4) * 4 + zh * 2 + core
        return reduce_copy(chunk, i, x_out.at[chunk, i - 1], x_in.at[chunk, i - 1], device)

    def z_copy(chunk):
        return reduce_copy(chunk, 4, z_out.at[chunk], z_in.at[chunk], z_mate)

    def core_stage(chunk):
        def part_step(index, _):
            core_out[chunk, index] = grad[chunk, 2 * index + 1 - core].astype(BF16)
            return 0

        lax.fori_loop(0, 8, part_step, 0)
        core_copy(chunk).start()

    def x_stage(chunk):
        core_copy(chunk).wait_recv()
        for i in (1, 2, 3):
            for half in (0, 1):
                j = 2 * ((x + i) % 4) + half
                x_out[chunk, i - 1, half] = (
                    grad[chunk, 2 * j + core] + core_in[chunk, j].astype(F32)
                ).astype(BF16)
            x_copy(chunk, i).start()

    def x_total(chunk, half):
        j = 2 * x + half
        total = grad[chunk, 2 * j + core] + core_in[chunk, j].astype(F32)
        for i in range(3):
            total = total + x_in[chunk, i, half].astype(F32)
        return total

    def z_stage(chunk):
        for i in (1, 2, 3):
            x_copy(chunk, i).wait_recv()
        z_out[chunk] = x_total(chunk, 1 - zh).astype(BF16)
        z_copy(chunk).start()

    def z_finish(chunk):
        z_copy(chunk).wait_recv()
        taps_grad[:, chunk * HALF : (chunk + 1) * HALF] = x_total(chunk, zh) + z_in[chunk].astype(F32)

    def first_transform(index, _):
        part_transform(0, index)
        return 0

    lax.fori_loop(0, blocks, first_transform, 0)
    mix_conv(0)
    back_conv(0, False)
    mix_grad()
    back_grad(0)
    core_stage(0)

    for far in (3, 2, 1, 0):

        def await_late(index, _):
            step = ranks - 1 - index
            late_copy(step, source_of(step)).wait_recv()
            conv_copy(0, target_of(step), ctx).start()
            return 0

        lax.fori_loop((3 - far) * side, min((4 - far) * side, ranks - 1), await_late, 0)
        from_z = (z + side - far) % side
        part_transform(1, 2 * from_z)
        part_transform(1, 2 * from_z + 1)

    x_stage(0)
    mix_conv(1)
    back_conv(1, True)
    z_stage(0)
    mix_grad()
    back_grad(1)
    core_stage(1)

    def gate_part(chunk, source, value):
        cols = pl.ds(pl.multiple_of((source * 2 + chunk) * HALF, HALF), HALF)
        mixed_own[:, cols] = (gate[:, cols] * value.astype(F32)).astype(BF16)

    def gate_step(chunk):
        def one(index, _):
            step = ranks - 1 - index
            source = source_of(step)
            conv_copy(chunk, target_of(1), source).wait_recv()
            gate_part(chunk, source, conv_in[source, chunk])
            return 0

        return one

    gate_part(0, ctx, conv_own[0, ctx])
    gate_part(1, ctx, conv_own[1, ctx])
    x_stage(1)
    lax.fori_loop(0, ranks - 1, gate_step(0), 0)
    z_stage(1)
    z_finish(0)
    stores = []
    for far in (3, 2, 1, 0):
        lax.fori_loop((3 - far) * side, min((4 - far) * side, ranks - 1), gate_step(1), 0)
        cols = pl.ds(pl.multiple_of(((z + side - far) % side) * group, group), group)
        stores.append(pltpu.make_async_copy(mixed_own.at[:, cols], mixed.at[:, cols], store_sems.at[far]))
        stores[-1].start()
    z_finish(1)

    halo_copy.wait_send()

    def drain_taps(step, _):
        taps_copy(dp, step, z_mate).wait_send()
        return 0

    lax.fori_loop(0, 15, drain_taps, 0)

    def drain_parts(step, _):
        body_copy(step, ctx).wait_send()
        head_copy(step, ctx).wait_send()
        late_copy(step, ctx).wait_send()
        for chunk in range(2):
            conv_copy(chunk, target_of(step), ctx).wait_send()
        return 0

    lax.fori_loop(1, ranks, drain_parts, 0)
    for chunk in range(2):
        core_copy(chunk).wait_send()
        for i in (1, 2, 3):
            x_copy(chunk, i).wait_send()
        z_copy(chunk).wait_send()
    for copy in stores:
        copy.wait()


def hand_over(mixed_in, grad_in, mixed, taps_grad, mixed_held, grad_held, load_sems, store_sems):
    parts = 4
    rows = mixed.shape[0] // parts
    loads = [pltpu.make_async_copy(grad_in, grad_held, load_sems.at[parts])]
    stores = [pltpu.make_async_copy(grad_held, taps_grad, store_sems.at[parts])]
    for part in range(parts):
        own = pl.ds(part * rows, rows)
        loads.append(pltpu.make_async_copy(mixed_in.at[own], mixed_held.at[own], load_sems.at[part]))
        stores.append(pltpu.make_async_copy(mixed_held.at[own], mixed.at[own], store_sems.at[part]))
    for load in loads:
        load.start()
    for load, store in zip(loads, stores):
        load.wait()
        store.start()
    for store in stores:
        store.wait()


def per_device(projected, short_weight, filter_taps, skip_gain, upstream):
    rows, joined = projected.shape[1:]
    width = joined // 3
    ranks = 16
    lanes = 2 * HALF
    blocks = ranks * rows // BLOCK
    forward, inverse = (jnp.asarray(t) for t in make_tables())
    vmem = pl.BlockSpec(memory_space=pltpu.VMEM)
    anywhere = pl.BlockSpec(memory_space=pl.ANY)
    shapes = [
        jax.ShapeDtypeStruct((rows, width), BF16),
        jax.ShapeDtypeStruct((rows, lanes), F32),
    ]
    results = pl.pallas_call(
        functools.partial(kernel, WINDOW),
        out_shape=shapes,
        in_specs=[anywhere, vmem, vmem, vmem, anywhere, anywhere, anywhere],
        out_specs=[anywhere, vmem],
        scratch_shapes=[
            pltpu.VMEM((rows, joined), BF16),
            pltpu.VMEM((rows, width), BF16),
            pltpu.VMEM(forward.shape, BF16),
            pltpu.VMEM(inverse.shape, BF16),
            pltpu.VMEM((16, joined), BF16),
            pltpu.VMEM((16, joined // 8), F32),
            pltpu.VMEM((16, joined // 8), BF16),
            pltpu.VMEM((16, joined // 8), BF16),
            pltpu.VMEM((8, joined), F32),
            pltpu.VMEM((rows, width), F32),
            pltpu.VMEM((rows, width), BF16),
            pltpu.VMEM((2, ranks, rows, lanes), BF16),
            pltpu.VMEM((2, ranks, rows, lanes), BF16),
            pltpu.VMEM((ranks, rows, lanes), BF16),
            pltpu.VMEM((blocks, 2 * BLOCK, lanes), F32),
            pltpu.VMEM((blocks, 2 * BLOCK, lanes), F32),
            pltpu.VMEM((blocks // 2, 2 * BLOCK, lanes), F32),
            pltpu.VMEM((2, ranks, rows, HALF), BF16),
            pltpu.VMEM((ranks, 2, rows, HALF), BF16),
            pltpu.VMEM((2, ranks, rows, HALF), F32),
            pltpu.VMEM((2, 8, rows, HALF), BF16),
            pltpu.VMEM((2, 8, rows, HALF), BF16),
            pltpu.VMEM((2, 3, 2, rows, HALF), BF16),
            pltpu.VMEM((2, 3, 2, rows, HALF), BF16),
            pltpu.VMEM((2, rows, HALF), BF16),
            pltpu.VMEM((2, rows, HALF), BF16),
            pltpu.SemaphoreType.DMA((4, 4)),
            pltpu.SemaphoreType.DMA((3,)),
            pltpu.SemaphoreType.DMA((4,)),
            pltpu.SemaphoreType.DMA((2,)),
            pltpu.SemaphoreType.DMA((16,)),
            pltpu.SemaphoreType.DMA((16,)),
            pltpu.SemaphoreType.DMA((16,)),
            pltpu.SemaphoreType.DMA((16,)),
            pltpu.SemaphoreType.DMA((2, 16)),
            pltpu.SemaphoreType.DMA((2, 16)),
            pltpu.SemaphoreType.DMA((2, 16)),
            pltpu.SemaphoreType.DMA((16, 2)),
            pltpu.SemaphoreType.DMA((2, 5)),
            pltpu.SemaphoreType.DMA((2, 5)),
        ],
        compiler_params=pltpu.CompilerParams(
            collective_id=0, has_side_effects=True, vmem_limit_bytes=60 * 2**20
        ),
    )(
        projected.reshape(rows, joined), short_weight, filter_taps, skip_gain.reshape(1, lanes),
        upstream.reshape(rows, width), forward, inverse,
    )
    mixed, taps_grad = pl.pallas_call(
        hand_over,
        out_shape=shapes,
        in_specs=[anywhere] * 2,
        out_specs=[anywhere] * 2,
        scratch_shapes=[
            pltpu.VMEM(shapes[0].shape, BF16),
            pltpu.VMEM(shapes[1].shape, F32),
            pltpu.SemaphoreType.DMA((5,)),
            pltpu.SemaphoreType.DMA((5,)),
        ],
        compiler_params=pltpu.CompilerParams(vmem_limit_bytes=60 * 2**20),
    )(*results)
    return (mixed.reshape(1, rows, width), taps_grad)


def solution(mesh):
    in_specs = (P("dp", "ctx", None), P(), P("dp", "ctx"), P("ctx"), P("dp", "ctx", None))
    out_specs = (P("dp", "ctx", None), P("dp", "ctx"))
    return jax.shard_map(
        per_device, mesh=mesh, in_specs=in_specs, out_specs=out_specs, check_vma=False
    )
```

time: 105 us -> 93.8 us (0.89)
  the two profiles are of different devices: /device:TPU:1 before, /device:TPU:24 now
where the time goes in v1:
time: 93.8 us; the launch traced here: 92.1 us
  Pallas kernels  91.5 us (98%)
    pallas_call x1, Pallas kernels, per_device(): pl.pallas_call(functools.partial(kernel, WINDOW), out_shape=shapes, in_sp...  89.4 us
    pallas_call x1, Pallas kernels, per_device(): pl.pallas_call(hand_over, out_shape=shapes, in_specs=[anywhere] * 2, out_...  2.07 us

profile of v1, /device:TPU:24, one launch (start us, length us, event | category | flops | bytes accessed | tf_op | source)
XLA Modules:
  0.0 92.1 jit_solution(6650159954505839358)
XLA Ops:
  0.6 89.4 %shard_map.86 = (bf16[128,4096]{1,0:T(8,128)(2,1)}, f32[128,256]{1,0:T(8,128)}) custom-call(bf16[128,12288]{1,0:T(8,128)(2,1)} %bitcast.4, f32[3,12288]{1,0:T(4,128)} %weights.1, f32[128,256]{1,0:T(8,128)} %taps.1, f32[1,256]{1,0:T(1,128)} %bitcast.6, bf16[128,4096]{1,0:T(8,128)(2,1)} %bitcast.5, bf16[2,512,256]{2,1,0:T(8,128)(2,1)} %constant.4.clone.forward_hbm, ...), custom_call_target="tpu_custom_call" | custom-call | tf_op jit(solution)/shard_map/pallas_call | solution.py:567
  90.0 2.1 %shard_map.87 = (bf16[128,4096]{1,0:T(8,128)(2,1)}, f32[128,256]{1,0:T(8,128)}) custom-call(bf16[128,4096]{1,0:T(8,128)(2,1)} %get-tuple-element.6.mixed_in, f32[128,256]{1,0:T(8,128)} %get-tuple-element.7.grad_in), custom_call_target="tpu_custom_call" | custom-call | tf_op jit(solution)/shard_map/pallas_call | solution.py:621

commit v2 on v1

--- a/solution.py
+++ b/solution.py
@@ -43,12 +43,12 @@
 
 
 def kernel(
-    window, proj_hbm, weights, taps, skip, upstream_hbm, forward_hbm, inverse_hbm,
+    window, proj_hbm, weights_hbm, taps_hbm, skip_hbm, upstream_hbm, forward_hbm, inverse_hbm,
     mixed, taps_grad,
-    proj, upstream, forward, inverse, tail, pack, halo_out, halo_in, halo, gate, mixed_own,
+    proj, upstream, weights, taps, skip, forward, inverse, tail, pack, halo_out, halo_in, halo, gate,
     outgoing, incoming, all_taps, taps_spec, spec, joint, conv_own, conv_in, grad,
     core_out, core_in, x_out, x_in, z_out, z_in,
-    load_sems, table_sems, store_sems, halo_sems, taps_send, taps_recv, head_send, head_recv,
+    load_sems, table_sems, halo_sems, taps_send, taps_recv, head_send, head_recv,
     part_send, part_recv, conv_send, conv_recv, red_send, red_recv,
 ):
     ctx, dp = lax.axis_index("ctx"), lax.axis_index("dp")
@@ -101,41 +101,38 @@
         )
         return copies
 
+    weights_load = pltpu.make_async_copy(weights_hbm, weights, table_sems.at[3])
+    weights_load.start()
+    for copy in loads_of(3):
+        copy.start()
     tail_load = pltpu.make_async_copy(proj_hbm.at[pl.ds(rows - 16, 16)], tail, table_sems.at[0])
     tail_load.start()
-    for far in (3, 2, 1, 0):
+    taps_load = pltpu.make_async_copy(taps_hbm, taps, table_sems.at[4])
+    taps_load.start()
+    for far in (2, 1, 0):
         for copy in loads_of(far):
             copy.start()
     table_loads = [
         pltpu.make_async_copy(forward_hbm, forward, table_sems.at[1]),
         pltpu.make_async_copy(inverse_hbm, inverse, table_sems.at[2]),
+        pltpu.make_async_copy(skip_hbm, skip, table_sems.at[5]),
     ]
     for copy in table_loads:
         copy.start()
 
-    all_taps[dp] = taps[...].astype(BF16)
-    tail_load.wait()
-    piece = 3 * width // 8
-    for seg in range(8):
-        last = tail[:, seg * piece : (seg + 1) * piece].astype(F32)
-        pack[2 * seg : 2 * seg + 2, :] = last[14:16]
-    halo_out[...] = pack[...].astype(BF16)
-
+    weights_load.wait()
     pl.semaphore_wait(barrier, ranks - 1 + 8)
 
     halo_copy = pltpu.make_async_remote_copy(
         src_ref=halo_out, dst_ref=halo_in, send_sem=halo_sems.at[0], recv_sem=halo_sems.at[1],
         device_id={"ctx": (ctx + 1) % ranks},
     )
-    halo_copy.start()
 
     def taps_copy(block, slot, target):
         return pltpu.make_async_remote_copy(
             src_ref=all_taps.at[block], dst_ref=all_taps.at[block],
             send_sem=taps_send.at[slot], recv_sem=taps_recv.at[block], device_id={"dp": target},
         )
-
-    taps_copy(dp, 0, z_mate).start()
 
     def body_copy(step, landing):
         body = pl.ds(16, rows - 16)
@@ -207,10 +204,21 @@
         body_copy(step, ctx).start()
         return 0
 
+    piece = 3 * width // 8
     for far in (3, 2, 1, 0):
         for copy in loads_of(far):
             copy.wait()
         lax.fori_loop((3 - far) * side, min((4 - far) * side, ranks - 1), send_body, 0)
+        if far == 3:
+            tail_load.wait()
+            for seg in range(8):
+                last = tail[:, seg * piece : (seg + 1) * piece].astype(F32)
+                pack[2 * seg : 2 * seg + 2, :] = last[14:16]
+            halo_out[...] = pack[...].astype(BF16)
+            halo_copy.start()
+            taps_load.wait()
+            all_taps[dp] = taps[...].astype(BF16)
+            taps_copy(dp, 0, z_mate).start()
     parts = make_parts(0, rows, filtered)
     incoming[0, ctx] = parts[0]
     incoming[1, ctx] = parts[1]
@@ -470,18 +478,20 @@
         from_z = (z + side - far) % side
         part_transform(1, 2 * from_z)
         part_transform(1, 2 * from_z + 1)
-
-    x_stage(0)
+        if far == 3:
+            x_stage(0)
+        if far == 1:
+            z_stage(0)
+
     mix_conv(1)
     back_conv(1, True)
-    z_stage(0)
     mix_grad()
     back_grad(1)
     core_stage(1)
 
     def gate_part(chunk, source, value):
         cols = pl.ds(pl.multiple_of((source * 2 + chunk) * HALF, HALF), HALF)
-        mixed_own[:, cols] = (gate[:, cols] * value.astype(F32)).astype(BF16)
+        mixed[:, cols] = (gate[:, cols] * value.astype(F32)).astype(BF16)
 
     def gate_step(chunk):
         def one(index, _):
@@ -495,18 +505,8 @@
 
     gate_part(0, ctx, conv_own[0, ctx])
     gate_part(1, ctx, conv_own[1, ctx])
+    z_finish(0)
     x_stage(1)
-    lax.fori_loop(0, ranks - 1, gate_step(0), 0)
-    z_stage(1)
-    z_finish(0)
-    stores = []
-    for far in (3, 2, 1, 0):
-        lax.fori_loop((3 - far) * side, min((4 - far) * side, ranks - 1), gate_step(1), 0)
-        cols = pl.ds(pl.multiple_of(((z + side - far) % side) * group, group), group)
-        stores.append(pltpu.make_async_copy(mixed_own.at[:, cols], mixed.at[:, cols], store_sems.at[far]))
-        stores[-1].start()
-    z_finish(1)
-
     halo_copy.wait_send()
 
     def drain_taps(step, _):
@@ -519,33 +519,37 @@
         body_copy(step, ctx).wait_send()
         head_copy(step, ctx).wait_send()
         late_copy(step, ctx).wait_send()
-        for chunk in range(2):
+        return 0
+
+    lax.fori_loop(1, ranks, drain_parts, 0)
+    z_stage(1)
+    lax.fori_loop(0, ranks - 1, gate_step(0), 0)
+
+    def drain_conv(chunk):
+        def one(step, _):
             conv_copy(chunk, target_of(step), ctx).wait_send()
-        return 0
-
-    lax.fori_loop(1, ranks, drain_parts, 0)
+            return 0
+
+        lax.fori_loop(1, ranks, one, 0)
+
+    drain_conv(0)
     for chunk in range(2):
         core_copy(chunk).wait_send()
         for i in (1, 2, 3):
             x_copy(chunk, i).wait_send()
-        z_copy(chunk).wait_send()
-    for copy in stores:
-        copy.wait()
-
-
-def hand_over(mixed_in, grad_in, mixed, taps_grad, mixed_held, grad_held, load_sems, store_sems):
-    parts = 4
-    rows = mixed.shape[0] // parts
-    loads = [pltpu.make_async_copy(grad_in, grad_held, load_sems.at[parts])]
-    stores = [pltpu.make_async_copy(grad_held, taps_grad, store_sems.at[parts])]
-    for part in range(parts):
-        own = pl.ds(part * rows, rows)
-        loads.append(pltpu.make_async_copy(mixed_in.at[own], mixed_held.at[own], load_sems.at[part]))
-        stores.append(pltpu.make_async_copy(mixed_held.at[own], mixed.at[own], store_sems.at[part]))
-    for load in loads:
-        load.start()
-    for load, store in zip(loads, stores):
-        load.wait()
+    z_copy(0).wait_send()
+    lax.fori_loop(0, ranks - 1, gate_step(1), 0)
+    drain_conv(1)
+    z_finish(1)
+    z_copy(1).wait_send()
+
+
+def hand_over(mixed_in, grad_in, mixed, taps_grad, sems):
+    stores = [
+        pltpu.make_async_copy(mixed_in, mixed, sems.at[0]),
+        pltpu.make_async_copy(grad_in, taps_grad, sems.at[1]),
+    ]
+    for store in stores:
         store.start()
     for store in stores:
         store.wait()
@@ -566,12 +570,15 @@
     ]
     results = pl.pallas_call(
         functools.partial(kernel, WINDOW),
-        out_shape=shapes,
-        in_specs=[anywhere, vmem, vmem, vmem, anywhere, anywhere, anywhere],
-        out_specs=[anywhere, vmem],
+        out_shape=[pltpu.VMEM(shape.shape, shape.dtype) for shape in shapes],
+        in_specs=[anywhere] * 7,
+        out_specs=[vmem] * 2,
         scratch_shapes=[
             pltpu.VMEM((rows, joined), BF16),
             pltpu.VMEM((rows, width), BF16),
+            pltpu.VMEM(short_weight.shape, F32),
+            pltpu.VMEM((rows, lanes), F32),
+            pltpu.VMEM((1, lanes), F32),
             pltpu.VMEM(forward.shape, BF16),
             pltpu.VMEM(inverse.shape, BF16),
             pltpu.VMEM((16, joined), BF16),
@@ -580,7 +587,6 @@
             pltpu.VMEM((16, joined // 8), BF16),
             pltpu.VMEM((8, joined), F32),
             pltpu.VMEM((rows, width), F32),
-            pltpu.VMEM((rows, width), BF16),
             pltpu.VMEM((2, ranks, rows, lanes), BF16),
             pltpu.VMEM((2, ranks, rows, lanes), BF16),
             pltpu.VMEM((ranks, rows, lanes), BF16),
@@ -597,8 +603,7 @@
             pltpu.VMEM((2, rows, HALF), BF16),
             pltpu.VMEM((2, rows, HALF), BF16),
             pltpu.SemaphoreType.DMA((4, 4)),
-            pltpu.SemaphoreType.DMA((3,)),
-            pltpu.SemaphoreType.DMA((4,)),
+            pltpu.SemaphoreType.DMA((6,)),
             pltpu.SemaphoreType.DMA((2,)),
             pltpu.SemaphoreType.DMA((16,)),
             pltpu.SemaphoreType.DMA((16,)),
@@ -621,15 +626,10 @@
     mixed, taps_grad = pl.pallas_call(
         hand_over,
         out_shape=shapes,
-        in_specs=[anywhere] * 2,
+        in_specs=[vmem] * 2,
         out_specs=[anywhere] * 2,
-        scratch_shapes=[
-            pltpu.VMEM(shapes[0].shape, BF16),
-            pltpu.VMEM(shapes[1].shape, F32),
-            pltpu.SemaphoreType.DMA((5,)),
-            pltpu.SemaphoreType.DMA((5,)),
-        ],
-        compiler_params=pltpu.CompilerParams(vmem_limit_bytes=60 * 2**20),
+        scratch_shapes=[pltpu.SemaphoreType.DMA((2,))],
+        compiler_params=pltpu.CompilerParams(vmem_limit_bytes=4 * 2**20),
     )(*results)
     return (mixed.reshape(1, rows, width), taps_grad)
 

time: 93.8 us -> 90.4 us (0.964); the launches traced: 92.1 us -> 90.3 us
  Pallas kernels: 91.5 us -> 89.7 us
    pallas_call x2, Pallas kernels: 91.5 us -> 89.7 us  [the longest x1 88.6 us: per_device(): pl.pallas_call(functools.partial(kernel, WINDOW), out_shape=[pltpu.VMEM(s...]
where the time goes in v2:
time: 90.4 us; the launch traced here: 90.3 us
  Pallas kernels  89.7 us (99%)
    pallas_call x1, Pallas kernels, per_device(): pl.pallas_call(functools.partial(kernel, WINDOW), out_shape=[pltpu.VMEM(s...  88.6 us

profile of v2, /device:TPU:24, one launch (start us, length us, event | category | flops | bytes accessed | tf_op | source)
XLA Modules:
  0.0 90.3 jit_solution(134722836842242229)
XLA Ops:
  0.6 88.6 %shard_map.86 = (bf16[128,4096]{1,0:T(8,128)(2,1)S(1)}, f32[128,256]{1,0:T(8,128)S(1)}) custom-call(bf16[128,12288]{1,0:T(8,128)(2,1)} %bitcast.4, f32[3,12288]{1,0:T(4,128)} %weights_hbm.1, f32[128,256]{1,0:T(8,128)} %taps_hbm.1, f32[1,256]{1,0:T(1,128)} %bitcast.6, bf16[128,4096]{1,0:T(8,128)(2,1)} %bitcast.5, ...), custom_call_target="tpu_custom_call" | custom-call | tf_op jit(solution)/shard_map/pallas_call | solution.py:571
  89.3 1.0 %shard_map.87 = (bf16[128,4096]{1,0:T(8,128)(2,1)}, f32[128,256]{1,0:T(8,128)}) custom-call(bf16[128,4096]{1,0:T(8,128)(2,1)S(1)} %get-tuple-element.6.mixed_in, f32[128,256]{1,0:T(8,128)S(1)} %get-tuple-element.7.grad_in), custom_call_target="tpu_custom_call" | custom-call | tf_op jit(solution)/shard_map/pallas_call | solution.py:626

commit v3 on v2

--- a/solution.py
+++ b/solution.py
@@ -247,8 +247,12 @@
     incoming[0, ctx, 0:16] = parts[0]
     incoming[1, ctx, 0:16] = parts[1]
 
+    def spread(index):
+        turn = index // 5
+        return jnp.where(index % 5 == 4, 3 - turn, ranks - 1 - index + turn)
+
     def send_late(index, _):
-        late_copy(ranks - 1 - index, ctx).start()
+        late_copy(spread(index), ctx).start()
         return 0
 
     def await_body(index, _):
@@ -377,18 +381,20 @@
         own = slice(chunk * HALF, (chunk + 1) * HALF)
 
         def pair_step(index, _):
-            pair = (z + side - 1 - index) % side
+            pair = (z + index) % side
             result = back(pair)
             for part in range(4):
                 target = 4 * pair + part
                 value = result[(part % 2) * HALF : (part % 2 + 1) * HALF, (part // 2) * HALF : (part // 2 + 1) * HALF]
                 product = incoming[chunk, target, :, 0:HALF].astype(F32)
                 conv_own[chunk, target] = (value + skip[:, own] * product).astype(BF16)
-                if send:
-
-                    @pl.when(target != ctx)
-                    def _():
-                        conv_copy(chunk, target, ctx).start()
+            if send:
+
+                @pl.when(index > 0)
+                def _():
+                    for part in range(4):
+                        conv_copy(chunk, 4 * pair + part, ctx).start()
+                    conv_copy(chunk, target_of(index), ctx).start()
 
             return 0
 
@@ -471,23 +477,26 @@
         def await_late(index, _):
             step = ranks - 1 - index
             late_copy(step, source_of(step)).wait_recv()
-            conv_copy(0, target_of(step), ctx).start()
+            if far:
+                conv_copy(0, target_of(step), ctx).start()
             return 0
 
         lax.fori_loop((3 - far) * side, min((4 - far) * side, ranks - 1), await_late, 0)
+        if far:
+            conv_copy(0, target_of(far), ctx).start()
         from_z = (z + side - far) % side
         part_transform(1, 2 * from_z)
         part_transform(1, 2 * from_z + 1)
         if far == 3:
             x_stage(0)
-        if far == 1:
-            z_stage(0)
 
     mix_conv(1)
     back_conv(1, True)
+    z_stage(0)
     mix_grad()
     back_grad(1)
     core_stage(1)
+    x_stage(1)
 
     def gate_part(chunk, source, value):
         cols = pl.ds(pl.multiple_of((source * 2 + chunk) * HALF, HALF), HALF)
@@ -503,10 +512,10 @@
 
         return one
 
+    z_stage(1)
     gate_part(0, ctx, conv_own[0, ctx])
     gate_part(1, ctx, conv_own[1, ctx])
     z_finish(0)
-    x_stage(1)
     halo_copy.wait_send()
 
     def drain_taps(step, _):
@@ -522,7 +531,6 @@
         return 0
 
     lax.fori_loop(1, ranks, drain_parts, 0)
-    z_stage(1)
     lax.fori_loop(0, ranks - 1, gate_step(0), 0)
 
     def drain_conv(chunk):

time: 90.4 us -> 89.1 us (0.986); the launches traced: 90.3 us -> 88.1 us
  Pallas kernels: 89.7 us -> 87.5 us
    pallas_call x1, Pallas kernels: 88.6 us -> 86.4 us  [per_device(): pl.pallas_call(functools.partial(kernel, WINDOW), out_shape=[pltpu.VMEM(s...]
where the time goes in v3:
time: 89.1 us; the launch traced here: 88.1 us
  Pallas kernels  87.5 us (98%)
    pallas_call x1, Pallas kernels, per_device(): pl.pallas_call(functools.partial(kernel, WINDOW), out_shape=[pltpu.VMEM(s...  86.4 us

profile of v3, /device:TPU:24, one launch (start us, length us, event | category | flops | bytes accessed | tf_op | source)
XLA Modules:
  0.0 88.1 jit_solution(2419991959289314994)
XLA Ops:
  0.6 86.4 %shard_map.86 = (bf16[128,4096]{1,0:T(8,128)(2,1)S(1)}, f32[128,256]{1,0:T(8,128)S(1)}) custom-call(bf16[128,12288]{1,0:T(8,128)(2,1)} %bitcast.4, f32[3,12288]{1,0:T(4,128)} %weights_hbm.1, f32[128,256]{1,0:T(8,128)} %taps_hbm.1, f32[1,256]{1,0:T(1,128)} %bitcast.6, bf16[128,4096]{1,0:T(8,128)(2,1)} %bitcast.5, ...), custom_call_target="tpu_custom_call" | custom-call | tf_op jit(solution)/shard_map/pallas_call | solution.py:579
  87.1 1.0 %shard_map.87 = (bf16[128,4096]{1,0:T(8,128)(2,1)}, f32[128,256]{1,0:T(8,128)}) custom-call(bf16[128,4096]{1,0:T(8,128)(2,1)S(1)} %get-tuple-element.6.mixed_in, f32[128,256]{1,0:T(8,128)S(1)} %get-tuple-element.7.grad_in), custom_call_target="tpu_custom_call" | custom-call | tf_op jit(solution)/shard_map/pallas_call | solution.py:634

commit v4 on v3

--- a/solution.py
+++ b/solution.py
@@ -227,7 +227,6 @@
         taps_copy(dp, step, plane_mate(step)).start()
         return 0
 
-    lax.fori_loop(1, 8, send_own, 0)
 
     halo_copy.wait_recv()
     pack[...] = jnp.where(ctx > 0, halo_in[...].astype(F32), 0.0)
@@ -272,9 +271,11 @@
         taps_copy(z_mate, 7 + step, plane_mate(step)).start()
         return 0
 
+
+    lax.fori_loop(window, 9, await_and_send, 0)
+    lax.fori_loop(1, 8, send_own, 0)
     lax.fori_loop(1, 8, forward_taps, 0)
-
-    lax.fori_loop(window, ranks - 1, await_and_send, 0)
+    lax.fori_loop(9, ranks - 1, await_and_send, 0)
 
     def await_taps(step, _):
         taps_copy(plane_mate(step), 0, z_mate).wait_recv()
@@ -553,10 +554,12 @@
 
 
 def hand_over(mixed_in, grad_in, mixed, taps_grad, sems):
-    stores = [
-        pltpu.make_async_copy(mixed_in, mixed, sems.at[0]),
-        pltpu.make_async_copy(grad_in, taps_grad, sems.at[1]),
-    ]
+    parts = 4
+    rows = mixed.shape[0] // parts
+    stores = [pltpu.make_async_copy(grad_in, taps_grad, sems.at[parts])]
+    for part in range(parts):
+        own = pl.ds(part * rows, rows)
+        stores.append(pltpu.make_async_copy(mixed_in.at[own], mixed.at[own], sems.at[part]))
     for store in stores:
         store.start()
     for store in stores:
@@ -636,7 +639,7 @@
         out_shape=shapes,
         in_specs=[vmem] * 2,
         out_specs=[anywhere] * 2,
-        scratch_shapes=[pltpu.SemaphoreType.DMA((2,))],
+        scratch_shapes=[pltpu.SemaphoreType.DMA((5,))],
         compiler_params=pltpu.CompilerParams(vmem_limit_bytes=4 * 2**20),
     )(*results)
     return (mixed.reshape(1, rows, width), taps_grad)

time: 89.1 us -> 89.2 us (level)
  no operation moved by 1% of the time
where the time goes in v4:
time: 89.2 us; the launch traced here: 88.1 us
  Pallas kernels  87.5 us (98%)
    pallas_call x1, Pallas kernels, per_device(): pl.pallas_call(functools.partial(kernel, WINDOW), out_shape=[pltpu.VMEM(s...  86.4 us

profile of v4, /device:TPU:24, one launch (start us, length us, event | category | flops | bytes accessed | tf_op | source)
XLA Modules:
  0.0 88.1 jit_solution(8127394848737816111)
XLA Ops:
  0.6 86.4 %shard_map.86 = (bf16[128,4096]{1,0:T(8,128)(2,1)S(1)}, f32[128,256]{1,0:T(8,128)S(1)}) custom-call(bf16[128,12288]{1,0:T(8,128)(2,1)} %bitcast.4, f32[3,12288]{1,0:T(4,128)} %weights_hbm.1, f32[128,256]{1,0:T(8,128)} %taps_hbm.1, f32[1,256]{1,0:T(1,128)} %bitcast.6, bf16[128,4096]{1,0:T(8,128)(2,1)} %bitcast.5, ...), custom_call_target="tpu_custom_call" | custom-call | tf_op jit(solution)/shard_map/pallas_call | solution.py:582
  87.1 1.0 %shard_map.87 = (bf16[128,4096]{1,0:T(8,128)(2,1)}, f32[128,256]{1,0:T(8,128)}) custom-call(bf16[128,4096]{1,0:T(8,128)(2,1)S(1)} %get-tuple-element.6.mixed_in, f32[128,256]{1,0:T(8,128)S(1)} %get-tuple-element.7.grad_in), custom_call_target="tpu_custom_call" | custom-call | tf_op jit(solution)/shard_map/pallas_call | solution.py:637

commit v5 on v3

--- a/solution.py
+++ b/solution.py
@@ -81,9 +81,6 @@
         pl.semaphore_signal(barrier, inc=1, device_id={"dp": plane_mate(step)})
         return 0
 
-    lax.fori_loop(1, ranks, greet, 0)
-    lax.fori_loop(1, 8, greet_plane, 0)
-    pl.semaphore_signal(barrier, inc=1, device_id={"dp": z_mate})
 
     group = side * lanes
 
@@ -105,6 +102,9 @@
     weights_load.start()
     for copy in loads_of(3):
         copy.start()
+    lax.fori_loop(1, ranks, greet, 0)
+    lax.fori_loop(1, 8, greet_plane, 0)
+    pl.semaphore_signal(barrier, inc=1, device_id={"dp": z_mate})
     tail_load = pltpu.make_async_copy(proj_hbm.at[pl.ds(rows - 16, 16)], tail, table_sems.at[0])
     tail_load.start()
     taps_load = pltpu.make_async_copy(taps_hbm, taps, table_sems.at[4])

time: 89.1 us -> 89.1 us (level)
  no operation moved by 1% of the time
where the time goes in v5:
time: 89.1 us; the launch traced here: 88.1 us
  Pallas kernels  87.5 us (98%)
    pallas_call x1, Pallas kernels, per_device(): pl.pallas_call(functools.partial(kernel, WINDOW), out_shape=[pltpu.VMEM(s...  86.4 us

profile of v5, /device:TPU:24, one launch (start us, length us, event | category | flops | bytes accessed | tf_op | source)
XLA Modules:
  0.0 88.1 jit_solution(2346060980434803366)
XLA Ops:
  0.6 86.4 %shard_map.86 = (bf16[128,4096]{1,0:T(8,128)(2,1)S(1)}, f32[128,256]{1,0:T(8,128)S(1)}) custom-call(bf16[128,12288]{1,0:T(8,128)(2,1)} %bitcast.4, f32[3,12288]{1,0:T(4,128)} %weights_hbm.1, f32[128,256]{1,0:T(8,128)} %taps_hbm.1, f32[1,256]{1,0:T(1,128)} %bitcast.6, bf16[128,4096]{1,0:T(8,128)(2,1)} %bitcast.5, ...), custom_call_target="tpu_custom_call" | custom-call | tf_op jit(solution)/shard_map/pallas_call | solution.py:579
  87.1 1.0 %shard_map.87 = (bf16[128,4096]{1,0:T(8,128)(2,1)}, f32[128,256]{1,0:T(8,128)}) custom-call(bf16[128,4096]{1,0:T(8,128)(2,1)S(1)} %get-tuple-element.6.mixed_in, f32[128,256]{1,0:T(8,128)S(1)} %get-tuple-element.7.grad_in), custom_call_target="tpu_custom_call" | custom-call | tf_op jit(solution)/shard_map/pallas_call | solution.py:634
